TPU v7x, 32 devices: a whole 2x2x4 slice. The times are simulated.
32 devices in a mesh: pair: 16 (over z, y, x), sector: 2 (over core).
Axes of the slice: x: 2, y: 2, z: 4, core: 2. Of those that a mesh axis runs over, the one named last changes fastest.
Arguments:
- site_tensor: bfloat16 [4, 16, 128, 128], P(None, 'sector', 'pair'), may hold values from -0.5 to 0.5
- operators: bfloat16 [384, 16, 128, 128], P('pair', 'sector'), may hold values from -6 to 6
- one_index: bfloat16 [32, 16, 128, 128], P('pair', 'sector'), may hold values from -6 to 6
- weights: bfloat16 [384, 32], P('pair'), may hold values from -2 to 2
- comp_charge: int32 [384], P('pair'), may hold values from 0 to 2
- one_charge: int32 [32], replicated, may hold values from 0 to 2
- sector_size: int32 [16], replicated, may hold values from 1 to 128, 1280 in all
- coupling: int32 [16, 4], replicated, may hold values from 0 to 16, as said below
Outputs:
- renormalized: bfloat16 [384, 16, 128, 128], P('pair', 'sector')
Inputs may be any that keep to these rules, and one draw needn't show every extreme that they name: coupling[s, t] = min(s + c[t], 16) where c is an arrangement of the charges 0, 1, 1, 2 over the 4 orbital states; the value 16 marks a dropped combination.
All inputs are finite; a program needn't handle non-finite values.
Results may differ from a plain program's by a relative error of at most 0.007.
Values may be sent and summed in bfloat16 or wider, within the bound.
A program may use at most 128 MiB of HBM per device.

v0:
```python
import jax
import jax.numpy as jnp
from jax import lax
from jax.experimental import pallas as pl
from jax.experimental.pallas import tpu as pltpu
from jax.sharding import PartitionSpec as P

ROWS = 16
REACH = 2


def from_behind(value, axis, steps):
    count = lax.axis_size(axis)
    initial, last = (max(0, -steps), min(count, count - steps))
    return lax.ppermute(value, axis, [(source, source + steps) for source in range(initial, last)])


def renormalize(sec_local, charge, shift, ops, ones, kron, pool, left, out, carry, comb, inner):
    step = pl.program_id(0)
    count, _, size, _ = ops.shape
    one_count = ones.shape[0]
    states = left.shape[0]

    @pl.when(step < sec_local)
    def _():
        for base in range(0, size, 2 * ROWS):
            rows = jnp.concatenate(
                [
                    ones[:, 0, start : start + ROWS, :].reshape(one_count * ROWS, size)
                    for start in (base, base + ROWS)
                ],
                axis=1,
            )
            added = jnp.dot(kron[...], rows, preferred_element_type=jnp.float32)
            for half in range(2):
                start = base + half * ROWS
                part = added[:, half * size : (half + 1) * size].reshape(count, ROWS, size)
                comb[:, start : start + ROWS, :] = (
                    ops[:, 0, start : start + ROWS, :].astype(jnp.float32) + part
                ).astype(jnp.bfloat16)
        slot = lax.rem(step, REACH + 1)

        def one(k, _):
            right = pool[step + charge[k]]
            value = jnp.dot(comb[k], right, preferred_element_type=jnp.float32)
            inner[slot, k] = value.astype(jnp.bfloat16)
            return 0

        lax.fori_loop(0, count, one, 0, unroll=4)

    lefts, slots = [], []
    for t in range(states):
        source = step - shift[t]
        legal = jnp.logical_and(source >= 0, source < sec_local)
        source = jnp.clip(source, 0, sec_local - 1)
        block = left[t, source]
        lefts.append(jnp.where(legal, block, jnp.zeros_like(block)))
        slots.append(lax.rem(source, REACH + 1))
    lhs = jnp.concatenate(lefts, axis=1)

    def emit(target):
        def two(pair, _):
            rhs = jnp.concatenate(
                [
                    jnp.concatenate(
                        [
                            inner[slots[t], 2 * pair + h, :, t * size : (t + 1) * size]
                            for t in range(states)
                        ],
                        axis=0,
                    )
                    for h in range(2)
                ],
                axis=1,
            )
            value = jnp.dot(lhs, rhs, preferred_element_type=jnp.float32)
            for h in range(2):
                target[2 * pair + h, 0] = value[:, h * size : (h + 1) * size].astype(jnp.bfloat16)
            return 0

        lax.fori_loop(0, count // 2, two, 0, unroll=2)

    @pl.when(step < sec_local)
    def _():
        emit(out)

    @pl.when(step >= sec_local)
    def _():
        emit(carry)


def body(
    site_tensor, operators, one_index, weights, comp_charge, one_charge, sector_size, coupling
):
    count, sec_local, size, _ = operators.shape
    states = site_tensor.shape[0]
    first_sector = lax.axis_index("sector") * sec_local
    gathered_site = lax.all_gather(site_tensor, "pair", axis=0)
    all_ones = lax.all_gather(one_index, "pair", axis=0, tiled=True)
    full_site = jnp.transpose(gathered_site, (1, 2, 0, 3, 4)).reshape(states, sec_local, size, size)
    own_sizes = lax.dynamic_slice_in_dim(sector_size, first_sector, sec_local)
    live_rows = jnp.arange(size, dtype=jnp.int32)[None, :] < own_sizes[:, None]
    own_site = jnp.where(live_rows[None, :, :, None], full_site, jnp.zeros((), jnp.bfloat16))
    upper = from_behind(own_site[:, :REACH], "sector", -1)
    pool = jnp.concatenate([own_site, upper], axis=1)
    pool = jnp.transpose(pool, (1, 2, 0, 3)).reshape(sec_local + REACH, size, states * size)
    left = jnp.swapaxes(own_site, 2, 3)
    matching = comp_charge[:, None] == one_charge[None, :]
    coef = jnp.where(matching, weights, jnp.zeros((), jnp.bfloat16))
    one_count = coef.shape[1]
    unit = jnp.eye(ROWS, dtype=jnp.bfloat16)
    kron = (coef[:, None, :, None] * unit[None, :, None, :]).reshape(
        count * ROWS, one_count * ROWS
    )

    def held(shape):
        return pl.BlockSpec(shape, lambda i, *_: (0,) * len(shape))

    def last(i):
        return jnp.minimum(i, sec_local - 1)

    out, carry = pl.pallas_call(
        lambda *refs: renormalize(sec_local, *refs),
        grid_spec=pltpu.PrefetchScalarGridSpec(
            num_scalar_prefetch=2,
            grid=(sec_local + REACH,),
            in_specs=[
                pl.BlockSpec((count, 1, size, size), lambda i, *_: (0, last(i), 0, 0)),
                pl.BlockSpec((one_count, 1, size, size), lambda i, *_: (0, last(i), 0, 0)),
                held(kron.shape),
                held(pool.shape),
                held(left.shape),
            ],
            out_specs=[
                pl.BlockSpec((count, 1, size, size), lambda i, *_: (0, last(i), 0, 0)),
                pl.BlockSpec(
                    (count, 1, size, size),
                    lambda i, *_: (0, jnp.maximum(i - sec_local, 0), 0, 0),
                ),
            ],
            scratch_shapes=[
                pltpu.VMEM((count, size, size), jnp.bfloat16),
                pltpu.VMEM((REACH + 1, count, size, states * size), jnp.bfloat16),
            ],
        ),
        out_shape=[
            jax.ShapeDtypeStruct(operators.shape, jnp.bfloat16),
            jax.ShapeDtypeStruct((count, REACH, size, size), jnp.bfloat16),
        ],
        compiler_params=pltpu.CompilerParams(vmem_limit_bytes=48 * 2**20),
    )(comp_charge, coupling[0], operators, all_ones, kron, pool, left)
    carried = from_behind(carry, "sector", 1)
    return out.at[:, :REACH].add(carried)


def solution(mesh):
    return jax.shard_map(
        body,
        mesh=mesh,
        in_specs=(
            P(None, "sector", "pair", None),
            P("pair", "sector", None, None),
            P("pair", "sector", None, None),
            P("pair", None),
            P("pair"),
            P(),
            P(),
            P(),
        ),
        out_specs=P("pair", "sector", None, None),
        check_vma=False,
    )
```

profile of v0, /device:TPU:13, one launch (start us, length us, event | category | flops | bytes accessed | tf_op | source)
XLA Modules:
  0.0 231.2 jit_solution(6983834206243178488)
XLA Ops:
  6.5 0.0 all-gather.6.cloned.1.call-start
  6.5 0.7 all-gather.6.cloned.1.call-update
  7.3 0.0 all-gather.4.cloned.1.call-start
  7.3 0.7 all-gather.4.cloned.1.call-update
  8.0 0.8 compare_select_fusion
  8.8 0.0 copy-start.2
  8.8 0.0 copy-start.1
  8.8 0.3 broadcast_multiply_fusion
  9.1 5.4 %mul.23.refs_4_ = bf16[384,512]{1,0:T(8,128)(2,1)S(1)} reshape(bf16[24,16,32,16]{3,2,1,0:T(8,128)(2,1)S(1)} %broadcast_multiply_fusion) | data formatting | bytes 786432 | tf_op jit(solution)/shard_map/mul | solution.py:112
  14.5 0.0 copy-done.2
  14.5 0.1 dynamic_slice.3
  14.6 0.0 copy-done.1
  14.6 0.1 slice_reduce_fusion.refs_1_
  14.7 0.1 iota_compare_fusion.1
  14.8 49.6 %all-gather.6.cloned.1.call-done = bf16[64,8,8,128]{3,2,1,0:T(8,128)(2,1)} async-done(((bf16[4,8,8,128]{3,2,1,0:T(8,128)(2,1)}), bf16[64,8,8,128]{3,2,1,0:T(8,128)(2,1)}) %all-gather.6.cloned.1.call-update) | async-done | bytes 1048592 | tf_op jit(solution)/shard_map/all_gather | solution.py:98
  64.3 1.5 copy.22
  65.8 0.7 copy.18
  66.5 0.1 broadcast_select_fusion
  66.6 3.9 %collective-permute-start = (bf16[4,2,128,128]{2,3,1,0:T(8,128)(2,1)S(1)}, bf16[4,2,128,128]{2,3,1,0:T(8,128)(2,1)S(1)}, u32[]{:S(2)}, u32[]{:S(2)}) collective-permute-start(bf16[4,2,128,128]{2,3,1,0:T(8,128)(2,1)S(1)} %slice.38), channel_id=1, source_target_pairs={{1,0},{3,2},{5,4},{7,6},{9,8},{11,10},{13,12},{15,14},{17,16},{19,... | collective-permute-start | bytes 786440 | tf_op jit(solution)/shard_map/ppermute | solution.py:15
  70.5 0.1 fusion.1.refs_6_
  70.6 1.0 collective-permute-done
  71.6 0.1 maximum_bitcast_fusion
  71.8 0.0 copy-start
  71.8 1.1 copy.19
  72.9 1.6 copy.20.refs_5_
  74.5 104.3 %all-gather.4.cloned.1.call-done.refs_3_ = bf16[32,8,128,128]{3,2,1,0:T(8,128)(2,1)} async-done(((bf16[2,8,128,128]{3,2,1,0:T(8,128)(2,1)}), bf16[32,8,128,128]{3,2,1,0:T(8,128)(2,1)}) %all-gather.4.cloned.1.call-update) | async-done | bytes 8388624 | tf_op jit(solution)/shard_map/all_gather | solution.py:99
  178.8 0.0 copy-done
  178.8 36.6 %shard_map.82 = (bf16[24,8,128,128]{3,2,1,0:T(8,128)(2,1)}, bf16[24,2,128,128]{3,2,1,0:T(8,128)(2,1)S(1)}) custom-call(s32[24]{0:T(128)S(1)} %copy-done, s32[4]{0:T(128)S(1)} %slice_reduce_fusion.refs_1_, bf16[24,8,128,128]{3,2,1,0:T(8,128)(2,1)} %refs_2_.1, bf16[32,8,128,128]{3,2,1,0:T(8,128)(2,1)} %all-gather.4.cloned.1.call-done.refs_3_, ...), custom_call_target="tpu_custom_call" | custom-call | tf_op jit(solution)/shard_map/pallas_call | solution.py:122
  215.4 1.3 collective-permute-start.1
  216.7 4.6 %collective-permute-done.1 = bf16[24,2,128,128]{3,2,1,0:T(8,128)(2,1)S(1)} collective-permute-done((bf16[24,2,128,128]{3,2,1,0:T(8,128)(2,1)S(1)}, bf16[24,2,128,128]{3,2,1,0:T(8,128)(2,1)S(1)}, u32[]{:S(2)}, u32[]{:S(2)}) %collective-permute-start.1) | collective-permute-done | bytes 1572896 | tf_op jit(solution)/shard_map/ppermute | solution.py:15
  221.2 3.1 %add_dynamic-update-slice_fusion = bf16[24,8,128,128]{3,2,1,0:T(8,128)(2,1)} fusion(bf16[24,8,128,128]{3,2,1,0:T(8,128)(2,1)} %get-tuple-element.19, bf16[24,2,128,128]{3,2,1,0:T(8,128)(2,1)S(1)} %collective-permute-done.1), kind=kLoop, calls=%fused_computation | loop fusion | flops 3145728 | bytes 4718592 | tf_op jit(solution)/shard_map/scatter-add | solution.py:153
  (2 shorter events, 0.0 us)
Async XLA Ops:
  6.5 57.8 %all-gather.6.cloned.1.call-start = ((), (), s32[]{:S(2)}) async-start(), calls=%async_computation.1 | async-start | bytes 1114112 | tf_op jit(solution)/shard_map/all_gather | solution.py:98
  7.3 171.5 %all-gather.4.cloned.1.call-start = ((), (), s32[]{:S(2)}) async-start(), calls=%async_computation | async-start | bytes 8912896 | tf_op jit(solution)/shard_map/all_gather | solution.py:99
  8.8 5.7 %copy-start.2 = (s32[16]{0:T(128)S(1)}, s32[16]{0:T(128)}, u32[]{:S(2)}) copy-start(s32[16]{0:T(128)} %param.16) | copy-start | bytes 196
  8.8 5.8 %copy-start.1 = (s32[16,4]{0,1:T(4,128)S(1)}, s32[16,4]{0,1:T(4,128)}, u32[]{:S(2)}) copy-start(s32[16,4]{0,1:T(4,128)} %param.17) | copy-start | bytes 772
  66.6 5.0 %collective-permute-start = (bf16[4,2,128,128]{2,3,1,0:T(8,128)(2,1)S(1)}, bf16[4,2,128,128]{2,3,1,0:T(8,128)(2,1)S(1)}, u32[]{:S(2)}, u32[]{:S(2)}) collective-permute-start(bf16[4,2,128,128]{2,3,1,0:T(8,128)(2,1)S(1)} %slice.38), channel_id=1, source_target_pairs={{1,0},{3,2},{5,4},{7,6},{9,8},{11,10},{13,12},{15,14},{17,16},{19,... | collective-permute-start | bytes 786440 | tf_op jit(solution)/shard_map/ppermute | solution.py:15
  71.8 107.0 %copy-start = (s32[24]{0:T(128)S(1)}, s32[24]{0:T(128)}, u32[]{:S(2)}) copy-start(s32[24]{0:T(128)} %refs_0_.1) | copy-start | bytes 292
  215.4 5.9 %collective-permute-start.1 = (bf16[24,2,128,128]{3,2,1,0:T(8,128)(2,1)S(1)}, bf16[24,2,128,128]{3,2,1,0:T(8,128)(2,1)S(1)}, u32[]{:S(2)}, u32[]{:S(2)}) collective-permute-start(bf16[24,2,128,128]{3,2,1,0:T(8,128)(2,1)S(1)} %get-tuple-element.20), channel_id=1, source_target_pairs={{0,1},{2,3},{4,5},{6,7},{8,9},{10,11},{12,13},{14,15},{16,17},{18,... | collective-permute-start | bytes 4718600 | tf_op jit(solution)/shard_map/ppermute | solution.py:15
Sparse Core Ops, SparseCore 0:
  10.1 54.1 all-gather.5
  67.1 111.6 all-gather.3
where the time goes:
time: 234 us; the launch traced here: 231 us
  waiting for transfers between devices  161 us (69%)
  Pallas kernels  36.6 us (16%)
  between operations  13.5 us (6%)
  local copies, waits for them, and re-layouts  10.5 us (4%)
  starting transfers between devices  5.18 us (2%)
  other arithmetic  4.54 us (2%)
    all_gather x1, waiting for transfers between devices, body(): all_ones = lax.all_gather(one_index, 'pair', axis=0, tiled=True)  104 us
    all_gather x1, waiting for transfers between devices, body(): gathered_site = lax.all_gather(site_tensor, 'pair', axis=0)  49.6 us
    pallas_call x1, Pallas kernels, body(): pl.pallas_call(lambda *refs: renormalize(sec_local, *refs), grid_spec=plt...  36.6 us
    ppermute x2, waiting for transfers between devices, from_behind(): lax.ppermute(value, axis, [(source, source + steps) for source in range(i...  5.63 us
    mul x1, local copies, waits for them, and re-layouts, body(): coef[:, None, :, None] * unit[None, :, None, :]  5.37 us
    ppermute x2, starting transfers between devices, from_behind(): lax.ppermute(value, axis, [(source, source + steps) for source in range(i...  5.14 us
  transfers between devices with their start and end apart: 4, of which 4 were waited for; matrix products, arithmetic and copies ran while one was open for 5% of the time, Pallas kernels for 0%

commit v1 on v0

--- a/solution.py
+++ b/solution.py
@@ -89,14 +89,146 @@
         emit(carry)
 
 
+def factors(count):
+    short = 1 << ((count.bit_length() - 1) // 3)
+    return (count // (short * short), short, short)
+
+
+def gather_both(dims, classes, site, ones, all_site, all_ones, send_sem, recv_sem, own_sem):
+    me = lax.axis_index("pair")
+    strides = (dims[1] * dims[2], dims[2], 1)
+    mine = [lax.rem(lax.div(me, strides[d]), dims[d]) for d in range(3)]
+
+    def moved(place, d, r):
+        other = lax.rem(mine[d] + r, dims[d])
+        return place + (other - mine[d]) * strides[d]
+
+    barrier = pltpu.get_barrier_semaphore()
+    greeted = 0
+    for d in range(3):
+        for r in range(1, dims[d]):
+            pl.semaphore_signal(
+                barrier,
+                inc=1,
+                device_id={"pair": moved(me, d, r)},
+                device_id_type=pl.DeviceIdType.MESH,
+            )
+            greeted += 1
+    keep = [
+        pltpu.make_async_copy(site, all_site.at[me], own_sem.at[0]),
+        pltpu.make_async_copy(ones, all_ones.at[me], own_sem.at[1]),
+    ]
+    for copy in keep:
+        copy.start()
+    pl.semaphore_wait(barrier, greeted)
+
+    sent = []
+
+    def piece(c, block, own):
+        slabs = classes[c][1]
+        if slabs is None:
+            return site if own else all_site.at[block]
+        part = pl.ds(*slabs)
+        return ones.at[part] if own else all_ones.at[block, part]
+
+    def send(c, block, own, stages):
+        for d in stages:
+            for r in range(1, dims[d]):
+                copy = pltpu.make_async_remote_copy(
+                    src_ref=piece(c, block, own),
+                    dst_ref=piece(c, block, False),
+                    send_sem=send_sem.at[len(sent)],
+                    recv_sem=recv_sem.at[c, block],
+                    device_id={"pair": moved(me, d, r)},
+                    device_id_type=pl.DeviceIdType.MESH,
+                )
+                copy.start()
+                sent.append(copy)
+
+    def arrive(c, block):
+        pltpu.make_async_remote_copy(
+            src_ref=piece(c, block, False),
+            dst_ref=piece(c, block, False),
+            send_sem=send_sem.at[0],
+            recv_sem=recv_sem.at[c, block],
+            device_id={"pair": moved(me, 2, 1)},
+            device_id_type=pl.DeviceIdType.MESH,
+        ).wait_recv()
+
+    for c, (order, _) in enumerate(classes):
+        send(c, me, True, order)
+    for stage in range(3):
+        rounds = []
+        for c, (order, _) in enumerate(classes):
+            steps = []
+            places = [me]
+            for d in order[:stage]:
+                places = [moved(p, d, r) for r in range(dims[d]) for p in places]
+            for r in range(1, dims[order[stage]]):
+                steps += [(c, moved(p, order[stage], r)) for p in places]
+            rounds.append(steps)
+        for i in range(max(len(steps) for steps in rounds)):
+            for steps in rounds:
+                if i < len(steps):
+                    c, block = steps[i]
+                    arrive(c, block)
+                    send(c, block, False, classes[c][0][stage + 1 :])
+    for copy in sent:
+        copy.wait_send()
+    for copy in keep:
+        copy.wait()
+
+
+def gather(site_tensor, one_index):
+    count = lax.axis_size("pair")
+    dims = factors(count)
+    size = site_tensor.shape[-1]
+    site = site_tensor.reshape(-1, size)
+    ones = one_index.reshape(-1, size, size)
+    slabs = ones.shape[0]
+    late = slabs // REACH // 8
+    early = (slabs - 2 * late) // 2
+    classes = [((0, 1, 2), None)]
+    first = 0
+    for order, number in (
+        ((0, 1, 2), early),
+        ((0, 2, 1), slabs - 2 * late - early),
+        ((2, 1, 0), late),
+        ((1, 2, 0), late),
+    ):
+        if number:
+            classes.append((order, (first, number)))
+        first += number
+    all_site, all_ones = pl.pallas_call(
+        lambda *refs: gather_both(dims, classes, *refs),
+        in_specs=[pl.BlockSpec(memory_space=pl.ANY)] * 2,
+        out_specs=[pl.BlockSpec(memory_space=pl.ANY)] * 2,
+        out_shape=[
+            jax.ShapeDtypeStruct((count,) + site.shape, site.dtype),
+            jax.ShapeDtypeStruct((count,) + ones.shape, ones.dtype),
+        ],
+        scratch_shapes=[
+            pltpu.SemaphoreType.DMA((len(classes) * (count - 1),)),
+            pltpu.SemaphoreType.DMA((len(classes), count)),
+            pltpu.SemaphoreType.DMA((2,)),
+        ],
+        compiler_params=pltpu.CompilerParams(
+            collective_id=0, has_side_effects=True, vmem_limit_bytes=48 * 2**20
+        ),
+    )(site, ones)
+    return (
+        all_site.reshape((count,) + site_tensor.shape),
+        all_ones.reshape((-1,) + one_index.shape[1:]),
+    )
+
+
 def body(
     site_tensor, operators, one_index, weights, comp_charge, one_charge, sector_size, coupling
 ):
     count, sec_local, size, _ = operators.shape
     states = site_tensor.shape[0]
     first_sector = lax.axis_index("sector") * sec_local
-    gathered_site = lax.all_gather(site_tensor, "pair", axis=0)
-    all_ones = lax.all_gather(one_index, "pair", axis=0, tiled=True)
+    gathered_site, all_ones = gather(site_tensor, one_index)
     full_site = jnp.transpose(gathered_site, (1, 2, 0, 3, 4)).reshape(states, sec_local, size, size)
     own_sizes = lax.dynamic_slice_in_dim(sector_size, first_sector, sec_local)
     live_rows = jnp.arange(size, dtype=jnp.int32)[None, :] < own_sizes[:, None]

time: 234 us -> 177 us (0.76)
  waiting for transfers between devices: 161 us -> 4.01 us
  Pallas kernels: 36.6 us -> 148 us
  between operations: 13.5 us -> 0.16 us
    all_gather x2 -> x0, waiting for transfers between devices: 154 us -> none  [the longest x1 104 us: body(): all_ones = lax.all_gather(one_index, 'pair', axis=0, tiled=True)]
    pallas_call x0 -> x1, Pallas kernels: none -> 111 us  [gather(): pl.pallas_call(lambda *refs: gather_both(dims, classes, *refs), in_specs=...]
  transfers between devices with their start and end apart: 4 -> 2, of which waited for: 4 -> 1; matrix products, arithmetic and copies ran while one was open for 5% -> 4% of each run, Pallas kernels for 0% -> 0%
where the time goes in v1:
time: 177 us; the launch traced here: 176 us
  Pallas kernels  148 us (84%)
  local copies, waits for them, and re-layouts  12.7 us (7%)
  other arithmetic  6.35 us (4%)
  starting transfers between devices  5.01 us (3%)
  waiting for transfers between devices  4.01 us (2%)
    pallas_call x1, Pallas kernels, gather(): pl.pallas_call(lambda *refs: gather_both(dims, classes, *refs), in_specs=...  111 us
    pallas_call x1, Pallas kernels, body(): pl.pallas_call(lambda *refs: renormalize(sec_local, *refs), grid_spec=plt...  36.7 us
    mul x1, local copies, waits for them, and re-layouts, body(): coef[:, None, :, None] * unit[None, :, None, :]  5.36 us
    ppermute x2, starting transfers between devices, from_behind(): lax.ppermute(value, axis, [(source, source + steps) for source in range(i...  5.01 us
    ppermute x2, waiting for transfers between devices, from_behind(): lax.ppermute(value, axis, [(source, source + steps) for source in range(i...  4.01 us
  transfers between devices with their start and end apart: 2, of which 1 were waited for; matrix products, arithmetic and copies ran while one was open for 4% of the time, Pallas kernels for 0%

profile of v1, /device:TPU:13, one launch (start us, length us, event | category | flops | bytes accessed | tf_op | source)
XLA Modules:
  0.0 176.3 jit_solution(6377887542270922002)
XLA Ops:
  0.0 0.7 dynamic_slice.3
  0.7 0.1 iota_compare_fusion.1
  0.8 1.0 copy-done
  1.8 0.8 copy-done.1
  2.7 111.4 %shard_map.82 = (bf16[16,256,128]{2,1,0:T(8,128)(2,1)S(1)}, bf16[16,16,128,128]{3,2,1,0:T(8,128)(2,1)}) custom-call(bf16[256,128]{1,0:T(8,128)(2,1)S(1)} %bitcast.18, bf16[16,128,128]{2,1,0:T(8,128)(2,1)S(1)} %bitcast.17), custom_call_target="tpu_custom_call" | custom-call | tf_op jit(solution)/shard_map/pallas_call | solution.py:202
  114.1 0.0 copy-start.6
  114.1 0.0 copy-start.2
  114.1 0.0 copy-start.5
  114.1 0.0 copy-start.7
  114.1 0.3 copy.15
  114.4 0.7 copy.11
  115.1 0.1 broadcast_select_fusion
  115.2 0.0 copy-start.4
  115.2 0.9 slice.38
  116.1 3.7 %collective-permute-start = (bf16[4,2,128,128]{2,3,1,0:T(8,128)(2,1)}, bf16[4,2,128,128]{2,3,1,0:T(8,128)(2,1)}, u32[]{:S(2)}, u32[]{:S(2)}) collective-permute-start(bf16[4,2,128,128]{2,3,1,0:T(8,128)(2,1)} %slice.38), channel_id=1, source_target_pairs={{1,0},{3,2},{5,4},{7,6},{9,8},{11,10},{13,12},{15,14},{17,16},{19,... | collective-permute-start | bytes 786440 | tf_op jit(solution)/shard_map/ppermute | solution.py:15
  119.8 0.0 copy-done.6
  119.8 0.1 slice_reduce_fusion.refs_1_
  119.9 0.0 copy-done.2
  119.9 0.0 copy-done.5
  119.9 0.0 copy-done.7
  120.0 0.1 compare_select_fusion
  120.0 0.3 broadcast_multiply_fusion
  120.3 5.4 %mul.23.refs_4_ = bf16[384,512]{1,0:T(8,128)(2,1)S(1)} reshape(bf16[24,16,32,16]{3,2,1,0:T(8,128)(2,1)S(1)} %broadcast_multiply_fusion) | data formatting | bytes 786432 | tf_op jit(solution)/shard_map/mul | solution.py:244
  125.7 1.3 fusion.1.refs_6_
  127.0 0.0 collective-permute-done
  127.0 1.4 maximum_bitcast_fusion
  128.4 1.1 copy.12
  129.6 1.6 copy.13.refs_5_
  131.2 36.7 %shard_map.83 = (bf16[24,8,128,128]{3,2,1,0:T(8,128)(2,1)}, bf16[24,2,128,128]{3,2,1,0:T(8,128)(2,1)S(1)}) custom-call(s32[24]{0:T(128)S(1)} %copy-done.2, s32[4]{0:T(128)S(1)} %slice_reduce_fusion.refs_1_, bf16[24,8,128,128]{3,2,1,0:T(8,128)(2,1)} %refs_2_.1, bf16[32,8,128,128]{3,2,1,0:T(8,128)(2,1)} %bitcast.19, bf16[384,512]{1,0:T(8,128)(2,1)S(1)} %mul.23.refs_4_, ...), custom_call_target="tpu_custom_call" | custom-call | tf_op jit(solution)/shard_map/pallas_call | solution.py:254
  167.9 1.3 collective-permute-start.1
  169.2 4.0 %collective-permute-done.1 = bf16[24,2,128,128]{3,2,1,0:T(8,128)(2,1)S(1)} collective-permute-done((bf16[24,2,128,128]{3,2,1,0:T(8,128)(2,1)S(1)}, bf16[24,2,128,128]{3,2,1,0:T(8,128)(2,1)S(1)}, u32[]{:S(2)}, u32[]{:S(2)}) %collective-permute-start.1) | collective-permute-done | bytes 1572896 | tf_op jit(solution)/shard_map/ppermute | solution.py:15
  173.2 3.1 %add_dynamic-update-slice_fusion = bf16[24,8,128,128]{3,2,1,0:T(8,128)(2,1)} fusion(bf16[24,8,128,128]{3,2,1,0:T(8,128)(2,1)} %get-tuple-element.23, bf16[24,2,128,128]{3,2,1,0:T(8,128)(2,1)S(1)} %collective-permute-done.1), kind=kLoop, calls=%fused_computation | loop fusion | flops 3145728 | bytes 4718592 | tf_op jit(solution)/shard_map/scatter-add | solution.py:285
  (6 shorter events, 0.0 us)
Async XLA Ops:
  0.8 1.0 copy-start
  1.8 0.8 copy-start.1
  114.1 5.8 %copy-start.6 = (s32[16,4]{0,1:T(4,128)S(1)}, s32[16,4]{0,1:T(4,128)}, u32[]{:S(2)}) copy-start(s32[16,4]{0,1:T(4,128)} %param.17) | copy-start | bytes 772
  114.1 5.9 %copy-start.2 = (s32[24]{0:T(128)S(1)}, s32[24]{0:T(128)}, u32[]{:S(2)}) copy-start(s32[24]{0:T(128)} %refs_0_.1) | copy-start | bytes 292
  114.1 5.9 %copy-start.5 = (bf16[24,32]{1,0:T(8,128)(2,1)S(1)}, bf16[24,32]{1,0:T(8,128)(2,1)}, u32[]{:S(2)}) copy-start(bf16[24,32]{1,0:T(8,128)(2,1)} %param.13) | copy-start | bytes 4612
  114.1 5.9 %copy-start.7 = (s32[32]{0:T(128)S(1)}, s32[32]{0:T(128)}, u32[]{:S(2)}) copy-start(s32[32]{0:T(128)} %param.15) | copy-start | bytes 388
  115.1 4.7 %copy-start.3 = (bf16[4,8,128,128]{2,3,1,0:T(8,128)(2,1)}, bf16[4,8,128,128]{2,3,1,0:T(8,128)(2,1)S(1)}, u32[]{:S(2)}) copy-start(bf16[4,8,128,128]{2,3,1,0:T(8,128)(2,1)S(1)} %copy.11) | copy-start | bytes 3145732
  115.2 4.8 %copy-start.4 = (bf16[4,8,128,128]{2,3,1,0:T(8,128)(2,1)}, bf16[4,8,128,128]{2,3,1,0:T(8,128)(2,1)S(1)}, u32[]{:S(2)}) copy-start(bf16[4,8,128,128]{2,3,1,0:T(8,128)(2,1)S(1)} %broadcast_select_fusion) | copy-start | bytes 3145732
  116.1 10.9 %collective-permute-start = (bf16[4,2,128,128]{2,3,1,0:T(8,128)(2,1)}, bf16[4,2,128,128]{2,3,1,0:T(8,128)(2,1)}, u32[]{:S(2)}, u32[]{:S(2)}) collective-permute-start(bf16[4,2,128,128]{2,3,1,0:T(8,128)(2,1)} %slice.38), channel_id=1, source_target_pairs={{1,0},{3,2},{5,4},{7,6},{9,8},{11,10},{13,12},{15,14},{17,16},{19,... | collective-permute-start | bytes 786440 | tf_op jit(solution)/shard_map/ppermute | solution.py:15
  167.9 5.3 %collective-permute-start.1 = (bf16[24,2,128,128]{3,2,1,0:T(8,128)(2,1)S(1)}, bf16[24,2,128,128]{3,2,1,0:T(8,128)(2,1)S(1)}, u32[]{:S(2)}, u32[]{:S(2)}) collective-permute-start(bf16[24,2,128,128]{3,2,1,0:T(8,128)(2,1)S(1)} %get-tuple-element.24), channel_id=1, source_target_pairs={{0,1},{2,3},{4,5},{6,7},{8,9},{10,11},{12,13},{14,15},{16,17},{18,... | collective-permute-start | bytes 4718600 | tf_op jit(solution)/shard_map/ppermute | solution.py:15

commit v2 on v1

--- a/solution.py
+++ b/solution.py
@@ -15,11 +15,29 @@
     return lax.ppermute(value, axis, [(source, source + steps) for source in range(initial, last)])
 
 
-def renormalize(sec_local, charge, shift, ops, ones, kron, pool, left, out, carry, comb, inner):
+def renormalize(sec_local, charge, shift, ops, ones, coef, pool, left, out, carry, kron, comb, inner):
     step = pl.program_id(0)
     count, _, size, _ = ops.shape
     one_count = ones.shape[0]
     states = left.shape[0]
+
+    @pl.when(step == 0)
+    def _():
+        def spread(shape, long, short):
+            far = lax.broadcasted_iota(jnp.int32, shape, long)
+            near = lax.broadcasted_iota(jnp.int32, shape, short) * ROWS
+            inside = jnp.logical_and(far >= near, far < near + ROWS)
+            return jnp.where(inside, 1.0, 0.0).astype(jnp.bfloat16)
+
+        tall = jnp.dot(
+            spread((count * ROWS, count), 0, 1), coef[...], preferred_element_type=jnp.float32
+        ).astype(jnp.bfloat16)
+        whole = jnp.dot(
+            tall, spread((one_count, one_count * ROWS), 1, 0), preferred_element_type=jnp.float32
+        )
+        row = lax.broadcasted_iota(jnp.int32, whole.shape, 0) & (ROWS - 1)
+        column = lax.broadcasted_iota(jnp.int32, whole.shape, 1) & (ROWS - 1)
+        kron[...] = jnp.where(row == column, whole, 0.0).astype(jnp.bfloat16)
 
     @pl.when(step < sec_local)
     def _():
@@ -187,12 +205,15 @@
     ones = one_index.reshape(-1, size, size)
     slabs = ones.shape[0]
     late = slabs // REACH // 8
-    early = (slabs - 2 * late) // 2
+    early = (slabs - 2 * late) // 4
+    rest = (slabs - 2 * late) // 2 - early
     classes = [((0, 1, 2), None)]
     first = 0
     for order, number in (
         ((0, 1, 2), early),
-        ((0, 2, 1), slabs - 2 * late - early),
+        ((0, 2, 1), early),
+        ((0, 1, 2), rest),
+        ((0, 2, 1), slabs - 2 * late - 2 * early - rest),
         ((2, 1, 0), late),
         ((1, 2, 0), late),
     ):
@@ -240,10 +261,6 @@
     matching = comp_charge[:, None] == one_charge[None, :]
     coef = jnp.where(matching, weights, jnp.zeros((), jnp.bfloat16))
     one_count = coef.shape[1]
-    unit = jnp.eye(ROWS, dtype=jnp.bfloat16)
-    kron = (coef[:, None, :, None] * unit[None, :, None, :]).reshape(
-        count * ROWS, one_count * ROWS
-    )
 
     def held(shape):
         return pl.BlockSpec(shape, lambda i, *_: (0,) * len(shape))
@@ -259,7 +276,7 @@
             in_specs=[
                 pl.BlockSpec((count, 1, size, size), lambda i, *_: (0, last(i), 0, 0)),
                 pl.BlockSpec((one_count, 1, size, size), lambda i, *_: (0, last(i), 0, 0)),
-                held(kron.shape),
+                held(coef.shape),
                 held(pool.shape),
                 held(left.shape),
             ],
@@ -271,6 +288,7 @@
                 ),
             ],
             scratch_shapes=[
+                pltpu.VMEM((count * ROWS, one_count * ROWS), jnp.bfloat16),
                 pltpu.VMEM((count, size, size), jnp.bfloat16),
                 pltpu.VMEM((REACH + 1, count, size, states * size), jnp.bfloat16),
             ],
@@ -280,7 +298,7 @@
             jax.ShapeDtypeStruct((count, REACH, size, size), jnp.bfloat16),
         ],
         compiler_params=pltpu.CompilerParams(vmem_limit_bytes=48 * 2**20),
-    )(comp_charge, coupling[0], operators, all_ones, kron, pool, left)
+    )(comp_charge, coupling[0], operators, all_ones, coef, pool, left)
     carried = from_behind(carry, "sector", 1)
     return out.at[:, :REACH].add(carried)
 

time: 177 us -> 167 us (0.944)
  local copies, waits for them, and re-layouts: 12.7 us -> 6.45 us
  other arithmetic: 6.35 us -> 3.52 us
    mul x1 -> x0, local copies, waits for them, and re-layouts: 5.36 us -> none  [body(): coef[:, None, :, None] * unit[None, :, None, :]]
  transfers between devices with their start and end apart: 2 -> 2, of which waited for: 1 -> 2; matrix products, arithmetic and copies ran while one was open for 4% -> 0% of each run, Pallas kernels for 0% -> 0%
where the time goes in v2:
time: 167 us; the launch traced here: 166 us
  Pallas kernels  147 us (88%)
  local copies, waits for them, and re-layouts  6.45 us (4%)
  waiting for transfers between devices  4.83 us (3%)
  starting transfers between devices  4.33 us (3%)
  other arithmetic  3.52 us (2%)
    pallas_call x1, Pallas kernels, gather(): pl.pallas_call(lambda *refs: gather_both(dims, classes, *refs), in_specs=...  110 us
    pallas_call x1, Pallas kernels, body(): pl.pallas_call(lambda *refs: renormalize(sec_local, *refs), grid_spec=plt...  37.1 us
    ppermute x2, waiting for transfers between devices, from_behind(): lax.ppermute(value, axis, [(source, source + steps) for source in range(i...  4.83 us
    ppermute x2, starting transfers between devices, from_behind(): lax.ppermute(value, axis, [(source, source + steps) for source in range(i...  4.33 us
  transfers between devices with their start and end apart: 2, of which 2 were waited for; matrix products, arithmetic and copies ran while one was open for 0% of the time, Pallas kernels for 0%

profile of v2, /device:TPU:13, one launch (start us, length us, event | category | flops | bytes accessed | tf_op | source)
XLA Modules:
  0.0 166.2 jit_solution(3787729743817196489)
XLA Ops:
  0.0 0.7 dynamic_slice.3
  0.7 0.1 iota_compare_fusion
  0.8 0.0 copy-start
  0.8 1.0 copy-done
  1.8 0.0 copy-start.1
  1.8 0.8 copy-done.1
  2.7 109.9 %shard_map.82 = (bf16[16,256,128]{2,1,0:T(8,128)(2,1)S(1)}, bf16[16,16,128,128]{3,2,1,0:T(8,128)(2,1)}) custom-call(bf16[256,128]{1,0:T(8,128)(2,1)S(1)} %bitcast.16, bf16[16,128,128]{2,1,0:T(8,128)(2,1)S(1)} %bitcast.15), custom_call_target="tpu_custom_call" | custom-call | tf_op jit(solution)/shard_map/pallas_call | solution.py:223
  112.6 0.3 copy.15
  112.8 0.7 copy.11
  113.5 0.0 copy-start.4
  113.5 0.0 copy-start.2
  113.5 0.0 copy-start.3
  113.5 0.0 copy-start.5
  113.6 0.1 broadcast_select_fusion
  113.7 3.0 %collective-permute-start = (bf16[4,2,128,128]{2,3,1,0:T(8,128)(2,1)S(1)}, bf16[4,2,128,128]{2,3,1,0:T(8,128)(2,1)S(1)}, u32[]{:S(2)}, u32[]{:S(2)}) collective-permute-start(bf16[4,2,128,128]{2,3,1,0:T(8,128)(2,1)S(1)} %slice.38), channel_id=1, source_target_pairs={{1,0},{3,2},{5,4},{7,6},{9,8},{11,10},{13,12},{15,14},{17,16},{19,... | collective-permute-start | bytes 786440 | tf_op jit(solution)/shard_map/ppermute | solution.py:15
  116.7 0.0 copy-done.4
  116.7 0.1 slice_reduce_fusion.refs_1_
  116.8 0.0 copy-done.2
  116.9 0.0 copy-done.3
  116.9 0.0 copy-done.5
  116.9 0.1 compare_select_fusion.refs_4_
  116.9 0.1 fusion.refs_6_
  117.0 0.8 collective-permute-done
  117.9 0.1 maximum_bitcast_fusion
  118.0 1.1 copy.12
  119.1 1.6 copy.13.refs_5_
  120.7 37.1 %shard_map.83 = (bf16[24,8,128,128]{3,2,1,0:T(8,128)(2,1)}, bf16[24,2,128,128]{3,2,1,0:T(8,128)(2,1)S(1)}) custom-call(s32[24]{0:T(128)S(1)} %copy-done.2, s32[4]{0:T(128)S(1)} %slice_reduce_fusion.refs_1_, bf16[24,8,128,128]{3,2,1,0:T(8,128)(2,1)} %refs_2_.1, bf16[32,8,128,128]{3,2,1,0:T(8,128)(2,1)} %bitcast.17, ...), custom_call_target="tpu_custom_call" | custom-call | tf_op jit(solution)/shard_map/pallas_call | solution.py:271
  157.8 1.3 collective-permute-start.1
  159.1 4.0 %collective-permute-done.1 = bf16[24,2,128,128]{3,2,1,0:T(8,128)(2,1)S(1)} collective-permute-done((bf16[24,2,128,128]{3,2,1,0:T(8,128)(2,1)S(1)}, bf16[24,2,128,128]{3,2,1,0:T(8,128)(2,1)S(1)}, u32[]{:S(2)}, u32[]{:S(2)}) %collective-permute-start.1) | collective-permute-done | bytes 1572896 | tf_op jit(solution)/shard_map/ppermute | solution.py:15
  163.1 3.1 %add_dynamic-update-slice_fusion = bf16[24,8,128,128]{3,2,1,0:T(8,128)(2,1)} fusion(bf16[24,8,128,128]{3,2,1,0:T(8,128)(2,1)} %get-tuple-element.23, bf16[24,2,128,128]{3,2,1,0:T(8,128)(2,1)S(1)} %collective-permute-done.1), kind=kLoop, calls=%fused_computation | loop fusion | flops 3145728 | bytes 4718592 | tf_op jit(solution)/shard_map/scatter-add | solution.py:303
  (1 shorter events, 0.0 us)
Async XLA Ops:
  0.8 1.0 copy-start
  1.8 0.8 copy-start.1
  113.5 3.2 %copy-start.4 = (s32[16,4]{0,1:T(4,128)S(1)}, s32[16,4]{0,1:T(4,128)}, u32[]{:S(2)}) copy-start(s32[16,4]{0,1:T(4,128)} %param.17) | copy-start | bytes 772
  113.5 3.3 %copy-start.2 = (s32[24]{0:T(128)S(1)}, s32[24]{0:T(128)}, u32[]{:S(2)}) copy-start(s32[24]{0:T(128)} %refs_0_.1) | copy-start | bytes 292
  113.5 3.3 %copy-start.3 = (bf16[24,32]{1,0:T(8,128)(2,1)S(1)}, bf16[24,32]{1,0:T(8,128)(2,1)}, u32[]{:S(2)}) copy-start(bf16[24,32]{1,0:T(8,128)(2,1)} %param.13) | copy-start | bytes 4612
  113.5 3.3 %copy-start.5 = (s32[32]{0:T(128)S(1)}, s32[32]{0:T(128)}, u32[]{:S(2)}) copy-start(s32[32]{0:T(128)} %param.15) | copy-start | bytes 388
  113.7 4.2 %collective-permute-start = (bf16[4,2,128,128]{2,3,1,0:T(8,128)(2,1)S(1)}, bf16[4,2,128,128]{2,3,1,0:T(8,128)(2,1)S(1)}, u32[]{:S(2)}, u32[]{:S(2)}) collective-permute-start(bf16[4,2,128,128]{2,3,1,0:T(8,128)(2,1)S(1)} %slice.38), channel_id=1, source_target_pairs={{1,0},{3,2},{5,4},{7,6},{9,8},{11,10},{13,12},{15,14},{17,16},{19,... | collective-permute-start | bytes 786440 | tf_op jit(solution)/shard_map/ppermute | solution.py:15
  157.8 5.3 %collective-permute-start.1 = (bf16[24,2,128,128]{3,2,1,0:T(8,128)(2,1)S(1)}, bf16[24,2,128,128]{3,2,1,0:T(8,128)(2,1)S(1)}, u32[]{:S(2)}, u32[]{:S(2)}) collective-permute-start(bf16[24,2,128,128]{3,2,1,0:T(8,128)(2,1)S(1)} %get-tuple-element.24), channel_id=1, source_target_pairs={{0,1},{2,3},{4,5},{6,7},{8,9},{10,11},{12,13},{14,15},{16,17},{18,... | collective-permute-start | bytes 4718600 | tf_op jit(solution)/shard_map/ppermute | solution.py:15

commit v3 on v2

--- a/solution.py
+++ b/solution.py
@@ -204,16 +204,13 @@
     site = site_tensor.reshape(-1, size)
     ones = one_index.reshape(-1, size, size)
     slabs = ones.shape[0]
-    late = slabs // REACH // 8
-    early = (slabs - 2 * late) // 4
-    rest = (slabs - 2 * late) // 2 - early
+    late = slabs // 8
+    early = (slabs - 2 * late) // 2
     classes = [((0, 1, 2), None)]
     first = 0
     for order, number in (
         ((0, 1, 2), early),
-        ((0, 2, 1), early),
-        ((0, 1, 2), rest),
-        ((0, 2, 1), slabs - 2 * late - 2 * early - rest),
+        ((0, 2, 1), slabs - 2 * late - early),
         ((2, 1, 0), late),
         ((1, 2, 0), late),
     ):

time: 167 us -> 162 us (0.970)
  Pallas kernels: 147 us -> 143 us
    pallas_call x1, Pallas kernels: 110 us -> 106 us  [gather(): pl.pallas_call(lambda *refs: gather_both(dims, classes, *refs), in_specs=...]
where the time goes in v3:
time: 162 us
  Pallas kernels  143 us (88%)
  local copies, waits for them, and re-layouts  6.45 us (4%)
  waiting for transfers between devices  4.83 us (3%)
  starting transfers between devices  4.33 us (3%)
  other arithmetic  3.52 us (2%)
    pallas_call x1, Pallas kernels, gather(): pl.pallas_call(lambda *refs: gather_both(dims, classes, *refs), in_specs=...  106 us
    pallas_call x1, Pallas kernels, body(): pl.pallas_call(lambda *refs: renormalize(sec_local, *refs), grid_spec=plt...  37.1 us
    ppermute x2, waiting for transfers between devices, from_behind(): lax.ppermute(value, axis, [(source, source + steps) for source in range(i...  4.83 us
    ppermute x2, starting transfers between devices, from_behind(): lax.ppermute(value, axis, [(source, source + steps) for source in range(i...  4.33 us
  transfers between devices with their start and end apart: 2, of which 2 were waited for; matrix products, arithmetic and copies ran while one was open for 0% of the time, Pallas kernels for 0%

profile of v3, /device:TPU:13, one launch (start us, length us, event | category | flops | bytes accessed | tf_op | source)
XLA Modules:
  0.0 162.1 jit_solution(5275207086992569075)
XLA Ops:
  0.0 0.7 dynamic_slice.3
  0.7 0.1 iota_compare_fusion
  0.8 0.0 copy-start
  0.8 1.0 copy-done
  1.8 0.0 copy-start.1
  1.8 0.8 copy-done.1
  2.7 105.7 %shard_map.82 = (bf16[16,256,128]{2,1,0:T(8,128)(2,1)S(1)}, bf16[16,16,128,128]{3,2,1,0:T(8,128)(2,1)}) custom-call(bf16[256,128]{1,0:T(8,128)(2,1)S(1)} %bitcast.16, bf16[16,128,128]{2,1,0:T(8,128)(2,1)S(1)} %bitcast.15), custom_call_target="tpu_custom_call" | custom-call | tf_op jit(solution)/shard_map/pallas_call | solution.py:220
  108.4 0.3 copy.15
  108.7 0.7 copy.11
  109.4 0.0 copy-start.4
  109.4 0.0 copy-start.2
  109.4 0.0 copy-start.3
  109.4 0.0 copy-start.5
  109.4 0.1 broadcast_select_fusion
  109.6 3.0 %collective-permute-start = (bf16[4,2,128,128]{2,3,1,0:T(8,128)(2,1)S(1)}, bf16[4,2,128,128]{2,3,1,0:T(8,128)(2,1)S(1)}, u32[]{:S(2)}, u32[]{:S(2)}) collective-permute-start(bf16[4,2,128,128]{2,3,1,0:T(8,128)(2,1)S(1)} %slice.38), channel_id=1, source_target_pairs={{1,0},{3,2},{5,4},{7,6},{9,8},{11,10},{13,12},{15,14},{17,16},{19,... | collective-permute-start | bytes 786440 | tf_op jit(solution)/shard_map/ppermute | solution.py:15
  112.6 0.0 copy-done.4
  112.6 0.1 slice_reduce_fusion.refs_1_
  112.7 0.0 copy-done.2
  112.7 0.0 copy-done.3
  112.7 0.0 copy-done.5
  112.8 0.1 compare_select_fusion.refs_4_
  112.8 0.1 fusion.refs_6_
  112.9 0.8 collective-permute-done
  113.7 0.1 maximum_bitcast_fusion
  113.9 1.1 copy.12
  115.0 1.6 copy.13.refs_5_
  116.6 37.1 %shard_map.83 = (bf16[24,8,128,128]{3,2,1,0:T(8,128)(2,1)}, bf16[24,2,128,128]{3,2,1,0:T(8,128)(2,1)S(1)}) custom-call(s32[24]{0:T(128)S(1)} %copy-done.2, s32[4]{0:T(128)S(1)} %slice_reduce_fusion.refs_1_, bf16[24,8,128,128]{3,2,1,0:T(8,128)(2,1)} %refs_2_.1, bf16[32,8,128,128]{3,2,1,0:T(8,128)(2,1)} %bitcast.17, ...), custom_call_target="tpu_custom_call" | custom-call | tf_op jit(solution)/shard_map/pallas_call | solution.py:268
  153.7 1.3 collective-permute-start.1
  155.0 4.0 %collective-permute-done.1 = bf16[24,2,128,128]{3,2,1,0:T(8,128)(2,1)S(1)} collective-permute-done((bf16[24,2,128,128]{3,2,1,0:T(8,128)(2,1)S(1)}, bf16[24,2,128,128]{3,2,1,0:T(8,128)(2,1)S(1)}, u32[]{:S(2)}, u32[]{:S(2)}) %collective-permute-start.1) | collective-permute-done | bytes 1572896 | tf_op jit(solution)/shard_map/ppermute | solution.py:15
  159.0 3.1 %add_dynamic-update-slice_fusion = bf16[24,8,128,128]{3,2,1,0:T(8,128)(2,1)} fusion(bf16[24,8,128,128]{3,2,1,0:T(8,128)(2,1)} %get-tuple-element.23, bf16[24,2,128,128]{3,2,1,0:T(8,128)(2,1)S(1)} %collective-permute-done.1), kind=kLoop, calls=%fused_computation | loop fusion | flops 3145728 | bytes 4718592 | tf_op jit(solution)/shard_map/scatter-add | solution.py:300
  (1 shorter events, 0.0 us)
Async XLA Ops:
  0.8 1.0 copy-start
  1.8 0.8 copy-start.1
  109.4 3.2 %copy-start.4 = (s32[16,4]{0,1:T(4,128)S(1)}, s32[16,4]{0,1:T(4,128)}, u32[]{:S(2)}) copy-start(s32[16,4]{0,1:T(4,128)} %param.17) | copy-start | bytes 772
  109.4 3.3 %copy-start.2 = (s32[24]{0:T(128)S(1)}, s32[24]{0:T(128)}, u32[]{:S(2)}) copy-start(s32[24]{0:T(128)} %refs_0_.1) | copy-start | bytes 292
  109.4 3.3 %copy-start.3 = (bf16[24,32]{1,0:T(8,128)(2,1)S(1)}, bf16[24,32]{1,0:T(8,128)(2,1)}, u32[]{:S(2)}) copy-start(bf16[24,32]{1,0:T(8,128)(2,1)} %param.13) | copy-start | bytes 4612
  109.4 3.3 %copy-start.5 = (s32[32]{0:T(128)S(1)}, s32[32]{0:T(128)}, u32[]{:S(2)}) copy-start(s32[32]{0:T(128)} %param.15) | copy-start | bytes 388
  109.6 4.2 %collective-permute-start = (bf16[4,2,128,128]{2,3,1,0:T(8,128)(2,1)S(1)}, bf16[4,2,128,128]{2,3,1,0:T(8,128)(2,1)S(1)}, u32[]{:S(2)}, u32[]{:S(2)}) collective-permute-start(bf16[4,2,128,128]{2,3,1,0:T(8,128)(2,1)S(1)} %slice.38), channel_id=1, source_target_pairs={{1,0},{3,2},{5,4},{7,6},{9,8},{11,10},{13,12},{15,14},{17,16},{19,... | collective-permute-start | bytes 786440 | tf_op jit(solution)/shard_map/ppermute | solution.py:15
  153.7 5.3 %collective-permute-start.1 = (bf16[24,2,128,128]{3,2,1,0:T(8,128)(2,1)S(1)}, bf16[24,2,128,128]{3,2,1,0:T(8,128)(2,1)S(1)}, u32[]{:S(2)}, u32[]{:S(2)}) collective-permute-start(bf16[24,2,128,128]{3,2,1,0:T(8,128)(2,1)S(1)} %get-tuple-element.24), channel_id=1, source_target_pairs={{0,1},{2,3},{4,5},{6,7},{8,9},{10,11},{12,13},{14,15},{16,17},{18,... | collective-permute-start | bytes 4718600 | tf_op jit(solution)/shard_map/ppermute | solution.py:15
